TPU v7x, 32 devices: a whole 2x2x4 slice. The times are simulated.
32 devices in a mesh: row: 4 (over z), col: 8 (over y, x, core).
Axes of the slice: x: 2, y: 2, z: 4, core: 2. Of those that a mesh axis runs over, the one named last changes fastest.
Arguments:
- right_side: float32 [4096, 4, 128], P(('row', 'col')), may hold values from -60 to 60
- cluster_of: int32 [4096], P(('row', 'col')), may hold values from 0 to 4095, as said below
- near_rows: int32 [12288], P(('row', 'col')), may hold values from 0 to 127
- near_columns: int32 [12288], P(('row', 'col')), may hold values from 0 to 191, as said below
- near_blocks: bfloat16 [12288, 128, 128], P(('row', 'col')), may hold values from -1 to 1
- far_rows: int32 [32768], P(('row', 'col')), may hold values from 0 to 1023, as said below
- far_columns: int32 [32768], P(('row', 'col')), may hold values from 0 to 511
- far_rank: int32 [32768], P(('row', 'col')), may hold values from 4 to 16
- far_left: bfloat16 [32768, 16, 128], P(('row', 'col')), may hold values from -1.5 to 1.5
- far_right: bfloat16 [32768, 16, 128], P(('row', 'col')), may hold values from -0.5 to 0.5
Outputs:
- second_basis: float32 [4096, 4, 128], P(('row', 'col'))
- next_vector: float32 [4096, 4, 128], P(('row', 'col'))
- hessenberg: float32 [5, 4], replicated
Inputs may be any that keep to these rules, and one draw needn't show every extreme that they name: `cluster_of`: A permutation of the cluster positions; position g belongs to the device of index g // 128 along row+col. Each device's blocks go to at most 8 blocks a destination device, and exactly 8 to some. `near_columns`: position 32 is the device's own first block; entries never point before the first or after the last block of cluster order. `far_rows`: in each device's list, the k-th group of 128 entries has rows in blocks k * 128 to (k + 1) * 128 - 1 of the row cluster.
All inputs are finite; a program needn't handle non-finite values.
Results may differ from a plain program's by a relative error of at most 0.0018.
The roundings to bfloat16 on the way count: a program that leaves them out, or rounds other values in their place, can miss the bound.
Values may be sent and summed in bfloat16 or wider, within the bound.
A program may use at most 128 MiB of HBM per device.

v0:
```python
import jax
import jax.numpy as jnp
from jax import lax
from jax.sharding import PartitionSpec as P

epsilon = 1e-06


def padded(cells, sides, width):
    for axis, dim in sides:
        count = lax.axis_size(axis)
        ends = count - 1
        head = lax.slice_in_dim(cells, 0, width, axis=dim)
        tail = lax.slice_in_dim(cells, cells.shape[dim] - width, cells.shape[dim], axis=dim)
        cells = jnp.concatenate(
            [
                lax.ppermute(tail, axis, [(i, (i + 1) % count) for i in range(ends)]),
                cells,
                lax.ppermute(head, axis, [((i + 1) % count, i) for i in range(ends)]),
            ],
            axis=dim,
        )
    return cells


def body(
    right_side,
    cluster_of,
    near_rows,
    near_columns,
    near_blocks,
    far_rows,
    far_columns,
    far_rank,
    far_left,
    far_right,
):
    row_count = lax.axis_size("row")
    column_count = lax.axis_size("col")
    device_count = row_count * column_count
    local_blocks = right_side.shape[0]
    sides = right_side.shape[1]
    width = right_side.shape[2]
    capacity = 2 * local_blocks // device_count
    halo_width = local_blocks // 4
    panels = local_blocks * device_count * width
    max_rank = far_left.shape[1]
    target = cluster_of // local_blocks
    place = cluster_of % local_blocks
    order = jnp.arange(local_blocks, dtype=jnp.int32)
    earlier = (target[None, :] == target[:, None]) & (order[None, :] < order[:, None])
    slot_index = jnp.sum(earlier.astype(jnp.int32), axis=1)
    position_send = (
        jnp.full((device_count, capacity), local_blocks, jnp.int32)
        .at[target, slot_index]
        .set(place)
    )
    position_recv = lax.all_to_all(
        position_send, ("row", "col"), split_axis=0, concat_axis=0, tiled=True
    ).reshape(-1)
    fetch_index = jnp.minimum(position_recv, local_blocks - 1)
    rank_mask = (jnp.arange(max_rank, dtype=jnp.int32)[None, :] < far_rank[:, None]).astype(
        jnp.float32
    )[:, :, None]

    def relay_in(vector):
        rounded = vector.astype(jnp.bfloat16)
        outgoing = (
            jnp.zeros((device_count, capacity, sides, width), jnp.bfloat16)
            .at[target, slot_index]
            .set(rounded)
        )
        arrived = lax.all_to_all(outgoing, ("row", "col"), split_axis=0, concat_axis=0, tiled=True)
        arrived = arrived.reshape(device_count * capacity, sides, width)
        return (
            jnp.zeros((local_blocks, sides, width), jnp.bfloat16)
            .at[position_recv]
            .set(arrived, mode="drop")
        )

    def relay_out(image_sum):
        outgoing = image_sum[fetch_index].reshape(device_count, capacity, sides, width)
        returned = lax.all_to_all(outgoing, ("row", "col"), split_axis=0, concat_axis=0, tiled=True)
        return returned[target, slot_index]

    def apply_clustered(clustered):
        extended = padded(clustered, ((("row", "col"), 0),), halo_width)
        near_out = jnp.einsum(
            "ekp,eqp->eqk", near_blocks, extended[near_columns], preferred_element_type=jnp.float32
        )
        image_sum = 0.5 * clustered.astype(jnp.float32)
        image_sum = image_sum.at[near_rows].add(near_out)
        gathered = lax.all_gather(clustered, "row", axis=0, tiled=True)
        coefficients = jnp.einsum(
            "etp,eqp->etq", far_right, gathered[far_columns], preferred_element_type=jnp.float32
        )
        coefficients = (coefficients * rank_mask).astype(jnp.bfloat16)
        far_out = jnp.einsum(
            "etq,etk->eqk", coefficients, far_left, preferred_element_type=jnp.float32
        )
        partial_value = (
            jnp.zeros((local_blocks * column_count, sides, width), jnp.float32)
            .at[far_rows]
            .add(far_out)
        )
        image_sum = image_sum + lax.psum_scatter(
            partial_value, "col", scatter_dimension=0, tiled=True
        )
        return image_sum

    def operate_mesh(vector):
        return relay_out(apply_clustered(relay_in(vector)))

    def local_inner(left_vector, right_vector):
        return jnp.sum(left_vector * right_vector, axis=(0, 2))

    side_norm = jnp.sqrt(
        lax.psum(local_inner(right_side, right_side), ("row", "col")) / panels + epsilon
    )
    first = right_side / side_norm[None, :, None]
    image_one = operate_mesh(first)
    project_one = lax.psum(local_inner(first, image_one), ("row", "col")) / panels
    remainder = image_one - project_one[None, :, None] * first
    norm_two = jnp.sqrt(
        lax.psum(local_inner(remainder, remainder), ("row", "col")) / panels + epsilon
    )
    second_basis = remainder / norm_two[None, :, None]
    image_two = operate_mesh(second_basis)
    sum_two, sum_three = lax.psum(
        (local_inner(first, image_two), local_inner(second_basis, image_two)), ("row", "col")
    )
    project_two = sum_two / panels
    project_three = sum_three / panels
    next_vector = (
        image_two - project_two[None, :, None] * first - project_three[None, :, None] * second_basis
    )
    second_basis, next_vector, entries = (
        second_basis,
        next_vector,
        (project_one, norm_two, project_two, project_three),
    )
    project_one, norm_two, project_two, project_three = entries
    hessenberg = jnp.stack([side_norm, project_one, norm_two, project_two, project_three])
    return (second_basis, next_vector, hessenberg)


def solution(mesh):
    placed = (
        P(("row", "col"), None, None),
        P(("row", "col")),
        P(("row", "col")),
        P(("row", "col")),
        P(("row", "col"), None, None),
        P(("row", "col")),
        P(("row", "col")),
        P(("row", "col")),
        P(("row", "col"), None, None),
        P(("row", "col"), None, None),
    )
    return jax.shard_map(
        body,
        mesh=mesh,
        in_specs=placed,
        out_specs=(P(("row", "col"), None, None), P(("row", "col"), None, None), P()),
        check_vma=False,
    )
```

profile of v0, /device:TPU:0, one launch (start us, length us, event | category | flops | bytes accessed | tf_op | source)
XLA Modules:
  0.0 642.0 jit_solution(10303565593195334214)
XLA Ops:
  7.2 0.7 and_select_fusion
  7.9 0.2 convert_reduce_fusion
  8.1 6.4 %scatter_fusion = s32[32,8]{0,1:T(8,128)S(1)} fusion(s32[32,8]{0,1:T(8,128)S(1)} %broadcast_in_dim.12, s32[128]{0:T(128)S(1)} %get-tuple-element.28, s32[128]{0:T(128)S(1)} %get-tuple-element.41), kind=kCustom, calls=%fused_computation.8 | custom fusion | bytes 2560 | tf_op jit(solution)/shard_map/scatter | solution.py:56
  14.5 0.7 copy.18
  15.2 7.3 %all-to-all-start = ((s32[32,1,8]{2,1,0:T(1,128)}), s32[32,1,8]{2,1,0:T(1,128)S(1)}, u32[]{:S(2)}, u32[]{:S(2)}) async-start(s32[32,1,8]{2,1,0:T(1,128)} %copy.18), calls=%async_computation | async-start | bytes 32768 | tf_op jit(solution)/shard_map/all_to_all | solution.py:58
  22.5 1.2 multiply_reduce_fusion.4
  23.7 0.7 compare_select_fusion.1
  24.4 40.5 %psum.35 = f32[4]{0:T(128)S(1)} all-reduce(f32[4]{0:T(128)S(1)} %multiply_reduce_fusion.4), channel_id=1, replica_groups=mesh['row'=4,'col'=8] {'row','col'}, use_global_device_ids=true, to_apply=%region_3.4 | all-reduce | flops 4 | bytes 32 | tf_op jit(solution)/shard_map/psum | solution.py:118
  64.9 1.1 fusion.17
  66.1 0.8 broadcast.143.clone
  66.8 14.8 %scatter_fusion.1 = bf16[32,8,4,128]{3,2,1,0:T(4,128)(2,1)} fusion(bf16[32,8,4,128]{3,2,1,0:T(4,128)(2,1)} %broadcast.143.clone, s32[128]{0:T(128)S(1)} %get-tuple-element.28, bf16[128,4,128]{2,1,0:T(4,128)(2,1)S(1)} %get-tuple-element.21), kind=kCustom, calls=%fused_computation.9 | custom fusion | bytes 394240 | tf_op jit(solution)/shard_map/scatter | solution.py:71
  81.6 4.5 all-to-all-start.1
  86.2 0.6 dynamic-slice
  87.4 0.2 fusion.4
  87.6 0.5 broadcast.352
  88.1 0.7 reduce.3
  88.9 7.8 %all-to-all-done.1 = bf16[32,8,4,128]{3,2,1,0:T(4,128)(2,1)S(1)} async-done(((bf16[32,8,4,128]{3,2,1,0:T(4,128)(2,1)}), bf16[32,8,4,128]{3,2,1,0:T(4,128)(2,1)S(1)}, u32[]{:S(2)}, u32[]{:S(2)}) %all-to-all-start.1) | async-done | bytes 262176 | tf_op jit(solution)/shard_map/all_to_all | solution.py:73
  96.7 7.3 %scatter_fusion.2 = bf16[128,4,128]{2,1,0:T(4,128)(2,1)S(1)} fusion(bf16[128,4,128]{2,1,0:T(4,128)(2,1)S(1)} %broadcast.137.clone, s32[256]{0:T(256)S(1)} %bitcast.57, bf16[256,4,128]{2,1,0:T(4,128)(2,1)S(1)} %bitcast.55), kind=kCustom, calls=%fused_computation.10 | custom fusion | bytes 787456 | tf_op jit(solution)/shard_map/scatter | solution.py:78
  104.1 15.9 %all_gather.6 = bf16[512,4,128]{2,1,0:T(4,128)(2,1)S(1)} all-gather(bf16[128,4,128]{2,1,0:T(4,128)(2,1)S(1)} %scatter_fusion.2), channel_id=1, replica_groups=mesh['row'=4,'col'=8] {'row'}, dimensions={0}, use_global_device_ids=true | all-gather | bytes 655360 | tf_op jit(solution)/shard_map/all_gather | solution.py:93
  120.0 3.6 gather_fusion
  123.5 8.3 %fusion = f32[1024,4,128]{2,1,0:T(4,128)} fusion(bf16[1024,16,128]{2,1,0:T(8,128)(2,1)} %param.18, bf16[1024,4,128]{2,1,0:T(4,128)(2,1)S(1)} %gather_fusion, bf16[1024,16,128]{2,1,0:T(8,128)(2,1)} %param.19, f32[1024,16]{1,0:T(8,128)S(1)} %fusion.4), kind=kOutput, calls=%fused_computation.19 | convolution fusion | flops 33685504 | bytes 11599872 | tf_op jit(solution)/shard_map/etq,etk->eqk/dot_general | solution.py:98
  131.8 0.3 broadcast.147.clone
  132.1 66.4 %scatter_fusion.3 = f32[1024,4,128]{2,1,0:T(4,128)S(1)} fusion(f32[1024,4,128]{2,1,0:T(4,128)S(1)} %broadcast.147.clone, s32[1024]{0:T(1024)S(1)} %compare_select_fusion.1, f32[1024,4,128]{2,1,0:T(4,128)} %fusion), kind=kCustom, calls=%fused_computation.11 | custom fusion | flops 524288 | bytes 6295552 | tf_op jit(solution)/shard_map/scatter-add | solution.py:104
  198.5 1.3 copy-done.1
  199.9 1.3 collective-permute-start.1
  201.2 3.0 collective-permute-start
  204.3 0.8 collective-permute-done
  205.3 2.0 gather_fusion.1
  207.3 9.6 %fusion.20 = f32[384,4,128]{2,1,0:T(4,128)S(1)} fusion(bf16[384,4,128]{2,1,0:T(4,128)(2,1)S(1)} %gather_fusion.1, bf16[384,128,128]{2,1,0:T(8,128)(2,1)} %param.14), kind=kOutput, calls=%fused_computation.78 | convolution fusion | flops 50331648 | bytes 13762560 | tf_op jit(solution)/shard_map/ekp,eqp->eqk/dot_general | solution.py:88
  216.9 42.0 %all-reduce.6.cloned.1.call-done = f32[1024,4,128]{2,1,0:T(4,128)} async-done(((f32[1024,4,128]{2,1,0:T(4,128)}), f32[1024,4,128]{2,1,0:T(4,128)}) %all-reduce.6.cloned.1.call-update) | async-done | bytes 2097168
  258.9 1.0 dynamic-slice_add_fusion.1
  260.0 14.2 %scatter_fusion.4 = f32[128,4,128]{2,1,0:T(4,128)S(1)} fusion(f32[128,4,128]{2,1,0:T(4,128)S(1)} %dynamic-slice_add_fusion.1, s32[384]{0:T(512)S(1)} %compare_select_fusion.5, f32[384,4,128]{2,1,0:T(4,128)S(1)} %fusion.20), kind=kCustom, calls=%fused_computation.12 | custom fusion | flops 196608 | bytes 2360832 | tf_op jit(solution)/shard_map/scatter-add | solution.py:92
  274.2 1.0 gather_fusion.2
  275.2 19.2 %all_to_all.29 = f32[32,8,4,128]{3,2,1,0:T(4,128)S(1)} all-to-all(f32[32,8,4,128]{3,2,1,0:T(4,128)S(1)} %bitcast.54), channel_id=1, replica_groups=mesh['row'=4,'col'=8] {'row','col'}, dimensions={0} | all-to-all | bytes 1048576 | tf_op jit(solution)/shard_map/all_to_all | solution.py:83
  294.4 0.9 gather_fusion.3
  295.4 0.3 multiply_reduce_fusion.3
  295.6 39.0 %psum.36 = f32[4]{0:T(128)S(1)} all-reduce(f32[4]{0:T(128)S(1)} %multiply_reduce_fusion.3), channel_id=1, replica_groups=mesh['row'=4,'col'=8] {'row','col'}, use_global_device_ids=true, to_apply=%region_10.11 | all-reduce | flops 4 | bytes 32 | tf_op jit(solution)/shard_map/psum | solution.py:122
  334.6 0.3 multiply_reduce_fusion.2
  334.9 40.0 %psum.37 = f32[4]{0:T(128)S(1)} all-reduce(f32[4]{0:T(128)S(1)} %multiply_reduce_fusion.2), channel_id=1, replica_groups=mesh['row'=4,'col'=8] {'row','col'}, use_global_device_ids=true, to_apply=%region_12.13 | all-reduce | flops 4 | bytes 32 | tf_op jit(solution)/shard_map/psum | solution.py:125
  375.0 0.2 fusion.16
  375.2 5.7 scatter_fusion.5
  380.9 14.6 %all_to_all.30 = bf16[32,8,4,128]{3,2,1,0:T(4,128)(2,1)S(1)} all-to-all(bf16[32,8,4,128]{3,2,1,0:T(4,128)(2,1)S(1)} %scatter_fusion.5), channel_id=1, replica_groups=mesh['row'=4,'col'=8] {'row','col'}, dimensions={0} | all-to-all | bytes 524288 | tf_op jit(solution)/shard_map/all_to_all | solution.py:73
  395.6 7.3 %scatter_fusion.6 = bf16[128,4,128]{2,1,0:T(4,128)(2,1)S(1)} fusion(bf16[128,4,128]{2,1,0:T(4,128)(2,1)S(1)} %broadcast.137, s32[256]{0:T(256)S(1)} %bitcast.58, bf16[256,4,128]{2,1,0:T(4,128)(2,1)S(1)} %bitcast.56), kind=kCustom, calls=%fused_computation.14 | custom fusion | bytes 787456 | tf_op jit(solution)/shard_map/scatter | solution.py:78
  402.9 15.9 %all_gather.7 = bf16[512,4,128]{2,1,0:T(4,128)(2,1)S(1)} all-gather(bf16[128,4,128]{2,1,0:T(4,128)(2,1)S(1)} %scatter_fusion.6), channel_id=1, replica_groups=mesh['row'=4,'col'=8] {'row'}, dimensions={0}, use_global_device_ids=true | all-gather | bytes 655360 | tf_op jit(solution)/shard_map/all_gather | solution.py:93
  418.8 3.6 gather_fusion.4
  422.4 8.3 %fusion.1 = f32[1024,4,128]{2,1,0:T(4,128)} fusion(bf16[1024,16,128]{2,1,0:T(8,128)(2,1)} %param.18, bf16[1024,4,128]{2,1,0:T(4,128)(2,1)S(1)} %gather_fusion.4, bf16[1024,16,128]{2,1,0:T(8,128)(2,1)} %param.19, f32[1024,16]{1,0:T(8,128)S(1)} %fusion.4), kind=kOutput, calls=%fused_computation.20 | convolution fusion | flops 33685504 | bytes 11599872 | tf_op jit(solution)/shard_map/etq,etk->eqk/dot_general | solution.py:98
  430.7 0.3 broadcast.147
  431.0 66.4 %scatter_fusion.7 = f32[1024,4,128]{2,1,0:T(4,128)S(1)} fusion(f32[1024,4,128]{2,1,0:T(4,128)S(1)} %broadcast.147, s32[1024]{0:T(1024)S(1)} %compare_select_fusion.1, f32[1024,4,128]{2,1,0:T(4,128)} %fusion.1), kind=kCustom, calls=%fused_computation.15 | custom fusion | flops 524288 | bytes 6295552 | tf_op jit(solution)/shard_map/scatter-add | solution.py:104
  497.4 1.3 copy-done
  498.8 1.3 collective-permute-start.3
  500.1 3.0 collective-permute-start.2
  503.1 0.8 collective-permute-done.2
  504.1 2.0 gather_fusion.5
  506.1 9.6 %fusion.21 = f32[384,4,128]{2,1,0:T(4,128)S(1)} fusion(bf16[384,4,128]{2,1,0:T(4,128)(2,1)S(1)} %gather_fusion.5, bf16[384,128,128]{2,1,0:T(8,128)(2,1)} %param.14), kind=kOutput, calls=%fused_computation.79 | convolution fusion | flops 50331648 | bytes 13762560 | tf_op jit(solution)/shard_map/ekp,eqp->eqk/dot_general | solution.py:88
  515.7 42.1 %all-reduce.8.cloned.1.call-done = f32[1024,4,128]{2,1,0:T(4,128)} async-done(((f32[1024,4,128]{2,1,0:T(4,128)}), f32[1024,4,128]{2,1,0:T(4,128)}) %all-reduce.8.cloned.1.call-update) | async-done | bytes 2097168
  557.8 1.0 dynamic-slice_add_fusion
  558.9 14.2 %scatter_fusion.8 = f32[128,4,128]{2,1,0:T(4,128)S(1)} fusion(f32[128,4,128]{2,1,0:T(4,128)S(1)} %dynamic-slice_add_fusion, s32[384]{0:T(512)S(1)} %compare_select_fusion.5, f32[384,4,128]{2,1,0:T(4,128)S(1)} %fusion.21), kind=kCustom, calls=%fused_computation.16 | custom fusion | flops 196608 | bytes 2360832 | tf_op jit(solution)/shard_map/scatter-add | solution.py:92
  573.1 1.0 gather_fusion.6
  574.1 19.2 %all_to_all.31 = f32[32,8,4,128]{3,2,1,0:T(4,128)S(1)} all-to-all(f32[32,8,4,128]{3,2,1,0:T(4,128)S(1)} %bitcast.53), channel_id=1, replica_groups=mesh['row'=4,'col'=8] {'row','col'}, dimensions={0} | all-to-all | bytes 1048576 | tf_op jit(solution)/shard_map/all_to_all | solution.py:83
  593.3 0.9 gather_fusion.7
  594.3 0.3 multiply_reduce_fusion.1
  594.6 39.0 %all-reduce.2 = (f32[4]{0:T(128)S(1)}, f32[4]{0:T(128)S(1)}) all-reduce(f32[4]{0:T(128)S(1)} %get-tuple-element.16, f32[4]{0:T(128)S(1)} %get-tuple-element.15), channel_id=1, replica_groups=mesh['row'=4,'col'=8] {'row','col'}, use_global_device_ids=true, to_apply=%region_21.22 | all-reduce | flops 8 | bytes 64 | tf_op jit(solution)/shard_map/psum | solution.py:129
  633.6 0.7 copy.19
  634.3 0.9 multiply_subtract_fusion
  (42 shorter events, 0.8 us)
Async XLA Ops:
  7.2 79.0 %copy-start.7 = (u32[32]{0:T(128)S(1)}, u32[32]{0:T(128)}, u32[]{:S(2)}) copy-start(u32[32]{0:T(128)} %constant.140) | copy-start | bytes 388
  7.2 58.8 %copy-start.4 = (s32[1024]{0:T(1024)S(1)}, s32[1024]{0:T(1024)}, u32[]{:S(2)}) copy-start(s32[1024]{0:T(1024)} %param.16) | copy-start | bytes 12292
  7.2 58.8 %copy-start.5 = (s32[384]{0:T(512)S(1)}, s32[384]{0:T(512)}, u32[]{:S(2)}) copy-start(s32[384]{0:T(512)} %param.12) | copy-start | bytes 4612
  7.2 58.8 %copy-start.6 = (s32[384]{0:T(512)S(1)}, s32[384]{0:T(512)}, u32[]{:S(2)}) copy-start(s32[384]{0:T(512)} %param.13) | copy-start | bytes 4612
  7.2 80.2 %copy-start.3 = (s32[1024]{0:T(1024)S(1)}, s32[1024]{0:T(1024)}, u32[]{:S(2)}) copy-start(s32[1024]{0:T(1024)} %param.17) | copy-start | bytes 12292
  15.2 66.4 %all-to-all-start = ((s32[32,1,8]{2,1,0:T(1,128)}), s32[32,1,8]{2,1,0:T(1,128)S(1)}, u32[]{:S(2)}, u32[]{:S(2)}) async-start(s32[32,1,8]{2,1,0:T(1,128)} %copy.18), calls=%async_computation | async-start | bytes 32768 | tf_op jit(solution)/shard_map/all_to_all | solution.py:58
  81.6 15.1 %all-to-all-start.1 = ((bf16[32,8,4,128]{3,2,1,0:T(4,128)(2,1)}), bf16[32,8,4,128]{3,2,1,0:T(4,128)(2,1)S(1)}, u32[]{:S(2)}, u32[]{:S(2)}) async-start(bf16[32,8,4,128]{3,2,1,0:T(4,128)(2,1)} %scatter_fusion.1), calls=%async_computation.1 | async-start | bytes 524288 | tf_op jit(solution)/shard_map/all_to_all | solution.py:73
  86.1 172.8 %all-reduce.6.cloned.1.call-start = ((), (), s32[]{:S(2)}) async-start(), calls=%async_computation.5 | async-start | bytes 4194304
  198.5 1.3 copy-start.1
  199.9 358.0 %all-reduce.8.cloned.1.call-start = ((), (), s32[]{:S(2)}) async-start(), calls=%async_computation.6 | async-start | bytes 4194304
  199.9 4.4 collective-permute-start.1
  201.2 3.9 collective-permute-start
  375.1 259.2 %copy-start.2 = (f32[128,4,128]{2,1,0:T(4,128)}, f32[128,4,128]{2,1,0:T(4,128)S(1)}, u32[]{:S(2)}) copy-start(f32[128,4,128]{2,1,0:T(4,128)S(1)} %get-tuple-element.20) | copy-start | bytes 786436
  497.4 1.3 copy-start
  498.8 4.3 collective-permute-start.3
  500.1 3.9 collective-permute-start.2
Sparse Core Ops, SparseCore 0:
  200.0 58.9 all-reduce.5
  498.8 58.9 all-reduce.7
where the time goes:
time: 652 us; the launch traced here: 642 us
  blocking collectives  243 us (37%)
  other arithmetic  170 us (26%)
  waiting for transfers between devices  93.6 us (14%)
  local copies, waits for them, and re-layouts  63.2 us (10%)
  matrix products  35.8 us (5%)
  starting transfers between devices  20.5 us (3%)
  between operations  15.1 us (2%)
    scatter-add x2, other arithmetic, apply_clustered(): partial_value = jnp.zeros((local_blocks * column_count, sides, width), jn...  133 us
    unnamed x4, waiting for transfers between devices  84.2 us
    psum x1, blocking collectives, body(): lax.psum(local_inner(right_side, right_side), ('row', 'col')) / panels  40.5 us
    psum x1, blocking collectives, body(): lax.psum(local_inner(remainder, remainder), ('row', 'col')) / panels  40 us
    psum x1, blocking collectives, body(): lax.psum(local_inner(first, image_one), ('row', 'col')) / panels  39 us
    psum x1, blocking collectives, body(): lax.psum((local_inner(first, image_two), local_inner(second_basis, image_...  39 us
    all_to_all x2, blocking collectives, relay_out(): lax.all_to_all(outgoing, ('row', 'col'), split_axis=0, concat_axis=0, til...  38.4 us
    all_gather x2, blocking collectives, apply_clustered(): gathered = lax.all_gather(clustered, 'row', axis=0, tiled=True)  31.8 us
  transfers between devices with their start and end apart: 8, of which 5 were waited for; matrix products, arithmetic and copies ran while one was open for 7% of the time, Pallas kernels for 0%

commit v1 on v0

--- a/solution.py
+++ b/solution.py
@@ -90,7 +90,13 @@
         )
         image_sum = 0.5 * clustered.astype(jnp.float32)
         image_sum = image_sum.at[near_rows].add(near_out)
-        gathered = lax.all_gather(clustered, "row", axis=0, tiled=True)
+        count_2 = lax.axis_size("row")
+        held, parts = (clustered, [clustered])
+        for _ in range(count_2 - 1):
+            held = lax.ppermute(held, "row", [(i_2, (i_2 + 1) % count_2) for i_2 in range(count_2)])
+            parts.insert(0, held)
+        merged = jnp.concatenate(parts, axis=0)
+        gathered = jnp.roll(merged, (lax.axis_index("row") + 1) * clustered.shape[0], axis=0)
         coefficients = jnp.einsum(
             "etp,eqp->etq", far_right, gathered[far_columns], preferred_element_type=jnp.float32
         )

time: 652 us -> 687 us (1.054)
  waiting for transfers between devices: 93.6 us -> 132 us
  blocking collectives: 243 us -> 211 us
  other arithmetic: 170 us -> 193 us
    ppermute x0 -> x6, waiting for transfers between devices: none -> 38.1 us  [apply_clustered(): lax.ppermute(held, 'row', [(i_2, (i_2 + 1) % count_2) for i_2 in range(co...]
    all_gather x2 -> x0, blocking collectives: 31.8 us -> none  [apply_clustered(): gathered = lax.all_gather(clustered, 'row', axis=0, tiled=True)]
    concatenate x0 -> x2, other arithmetic: none -> 23.4 us  [apply_clustered(): jnp.roll(merged, (lax.axis_index('row') + 1) * clustered.shape[0], axis=0)]
  transfers between devices with their start and end apart: 8 -> 14, of which waited for: 5 -> 11; matrix products, arithmetic and copies ran while one was open for 7% -> 6% of each run, Pallas kernels for 0% -> 0%
where the time goes in v1:
time: 687 us; the launch traced here: 674 us
  blocking collectives  211 us (31%)
  other arithmetic  193 us (28%)
  waiting for transfers between devices  132 us (19%)
  local copies, waits for them, and re-layouts  63.3 us (9%)
  matrix products  35.7 us (5%)
  starting transfers between devices  23 us (3%)
  between operations  15.4 us (2%)
    scatter-add x2, other arithmetic, apply_clustered(): partial_value = jnp.zeros((local_blocks * column_count, sides, width), jn...  133 us
    unnamed x4, waiting for transfers between devices  83.4 us
    psum x1, blocking collectives, body(): lax.psum(local_inner(right_side, right_side), ('row', 'col')) / panels  40.5 us
    psum x1, blocking collectives, body(): lax.psum(local_inner(remainder, remainder), ('row', 'col')) / panels  40 us
    psum x1, blocking collectives, body(): lax.psum((local_inner(first, image_two), local_inner(second_basis, image_...  39 us
    psum x1, blocking collectives, body(): lax.psum(local_inner(first, image_one), ('row', 'col')) / panels  39 us
    all_to_all x2, blocking collectives, relay_out(): lax.all_to_all(outgoing, ('row', 'col'), split_axis=0, concat_axis=0, til...  38.4 us
    ppermute x6, waiting for transfers between devices, apply_clustered(): lax.ppermute(held, 'row', [(i_2, (i_2 + 1) % count_2) for i_2 in range(co...  38.1 us
  transfers between devices with their start and end apart: 14, of which 11 were waited for; matrix products, arithmetic and copies ran while one was open for 6% of the time, Pallas kernels for 0%

profile of v1, /device:TPU:0, one launch (start us, length us, event | category | flops | bytes accessed | tf_op | source)
XLA Modules:
  0.0 674.2 jit_solution(13600605513830649070)
XLA Ops:
  7.2 0.7 and_select_fusion
  8.1 6.4 scatter_fusion
  14.6 0.7 copy.18
  15.2 1.2 multiply_reduce_fusion.4
  16.4 7.3 %all-to-all-start = ((s32[32,1,8]{2,1,0:T(1,128)}), s32[32,1,8]{2,1,0:T(1,128)S(1)}, u32[]{:S(2)}, u32[]{:S(2)}) async-start(s32[32,1,8]{2,1,0:T(1,128)} %copy.18), calls=%async_computation | async-start | bytes 32768 | tf_op jit(solution)/shard_map/all_to_all | solution.py:58
  23.7 40.5 %psum.35 = f32[4]{0:T(128)S(1)} all-reduce(f32[4]{0:T(128)S(1)} %multiply_reduce_fusion.4), channel_id=1, replica_groups=mesh['row'=4,'col'=8] {'row','col'}, use_global_device_ids=true, to_apply=%region_3.4 | all-reduce | flops 4 | bytes 32 | tf_op jit(solution)/shard_map/psum | solution.py:124
  64.3 1.1 fusion.31
  65.4 0.8 broadcast.147.clone
  66.1 14.8 %scatter_fusion.1 = bf16[32,8,4,128]{3,2,1,0:T(4,128)(2,1)} fusion(bf16[32,8,4,128]{3,2,1,0:T(4,128)(2,1)} %broadcast.147.clone, s32[128]{0:T(128)S(1)} %get-tuple-element.29, bf16[128,4,128]{2,1,0:T(4,128)(2,1)S(1)} %get-tuple-element.22), kind=kCustom, calls=%fused_computation.9 | custom fusion | bytes 394240 | tf_op jit(solution)/shard_map/scatter | solution.py:71
  80.9 4.5 all-to-all-start.1
  85.7 0.5 broadcast.357
  86.2 0.7 reduce.3
  87.0 9.0 %all-to-all-done.1 = bf16[32,8,4,128]{3,2,1,0:T(4,128)(2,1)S(1)} async-done(((bf16[32,8,4,128]{3,2,1,0:T(4,128)(2,1)}), bf16[32,8,4,128]{3,2,1,0:T(4,128)(2,1)S(1)}, u32[]{:S(2)}, u32[]{:S(2)}) %all-to-all-start.1) | async-done | bytes 262176 | tf_op jit(solution)/shard_map/all_to_all | solution.py:73
  96.0 7.3 %scatter_fusion.2 = bf16[128,4,128]{2,1,0:T(4,128)(2,1)S(1)} fusion(bf16[128,4,128]{2,1,0:T(4,128)(2,1)S(1)} %broadcast.140.clone, s32[256]{0:T(256)S(1)} %bitcast.57, bf16[256,4,128]{2,1,0:T(4,128)(2,1)S(1)} %bitcast.55), kind=kCustom, calls=%fused_computation.10 | custom fusion | bytes 787456 | tf_op jit(solution)/shard_map/scatter | solution.py:78
  103.4 1.0 collective-permute-start
  104.3 6.2 collective-permute-done
  110.5 6.8 %collective-permute-done.1 = bf16[128,4,128]{2,1,0:T(4,128)(2,1)S(1)} collective-permute-done((bf16[128,4,128]{2,1,0:T(4,128)(2,1)S(1)}, bf16[128,4,128]{2,1,0:T(4,128)(2,1)S(1)}, u32[]{:S(2)}, u32[]{:S(2)}) %collective-permute-start.1) | collective-permute-done | bytes 131104 | tf_op jit(solution)/shard_map/ppermute | solution.py:96
  117.5 0.6 dynamic-slice
  118.8 5.4 collective-permute-done.2
  124.2 11.7 %fusion.14 = bf16[512,4,128]{2,1,0:T(4,128)(2,1)S(1)} fusion(s32[]{:T(128)S(6)} %select_n.93, bf16[128,4,128]{2,1,0:T(4,128)(2,1)S(1)} %collective-permute-done.2, bf16[128,4,128]{2,1,0:T(4,128)(2,1)S(1)} %collective-permute-done.1, bf16[128,4,128]{2,1,0:T(4,128)(2,1)S(1)} %collective-permute-done, bf16[128,4,128]{2,1,0:T(4,128)(2,1)S(1)} %scatter_fusion.2), kind=kLoop, calls=%fused_computation.49 | loop fusion | flops 1835008 | bytes 1048580 | tf_op jit(solution)/shard_map/jit(_roll_dynamic)/concatenate | solution.py:99
  135.9 3.6 gather_fusion
  139.5 8.3 %fusion = f32[1024,4,128]{2,1,0:T(4,128)} fusion(bf16[1024,16,128]{2,1,0:T(8,128)(2,1)} %param.20, bf16[1024,4,128]{2,1,0:T(4,128)(2,1)S(1)} %gather_fusion, bf16[1024,16,128]{2,1,0:T(8,128)(2,1)} %param.21, f32[1024,16]{1,0:T(8,128)S(1)} %fusion.18), kind=kOutput, calls=%fused_computation.19 | convolution fusion | flops 33685504 | bytes 11599872 | tf_op jit(solution)/shard_map/etq,etk->eqk/dot_general | solution.py:104
  148.1 66.4 %scatter_fusion.3 = f32[1024,4,128]{2,1,0:T(4,128)S(1)} fusion(f32[1024,4,128]{2,1,0:T(4,128)S(1)} %broadcast.151.clone, s32[1024]{0:T(1024)S(1)} %compare_select_fusion.1, f32[1024,4,128]{2,1,0:T(4,128)} %fusion), kind=kCustom, calls=%fused_computation.11 | custom fusion | flops 524288 | bytes 6295552 | tf_op jit(solution)/shard_map/scatter-add | solution.py:110
  214.5 1.3 copy-done.1
  215.9 1.3 collective-permute-start.4
  217.2 3.0 collective-permute-start.3
  220.3 0.8 collective-permute-done.3
  221.2 2.0 gather_fusion.1
  223.3 9.6 %fusion.34 = f32[384,4,128]{2,1,0:T(4,128)S(1)} fusion(bf16[384,4,128]{2,1,0:T(4,128)(2,1)S(1)} %gather_fusion.1, bf16[384,128,128]{2,1,0:T(8,128)(2,1)} %param.16), kind=kOutput, calls=%fused_computation.108 | convolution fusion | flops 50331648 | bytes 13762560 | tf_op jit(solution)/shard_map/ekp,eqp->eqk/dot_general | solution.py:88
  232.8 41.7 %all-reduce.6.cloned.1.call-done = f32[1024,4,128]{2,1,0:T(4,128)} async-done(((f32[1024,4,128]{2,1,0:T(4,128)}), f32[1024,4,128]{2,1,0:T(4,128)}) %all-reduce.6.cloned.1.call-update) | async-done | bytes 2097168
  274.5 1.0 dynamic-slice_add_fusion.1
  275.5 14.2 %scatter_fusion.4 = f32[128,4,128]{2,1,0:T(4,128)S(1)} fusion(f32[128,4,128]{2,1,0:T(4,128)S(1)} %dynamic-slice_add_fusion.1, s32[384]{0:T(512)S(1)} %compare_select_fusion.5, f32[384,4,128]{2,1,0:T(4,128)S(1)} %fusion.34), kind=kCustom, calls=%fused_computation.12 | custom fusion | flops 196608 | bytes 2360832 | tf_op jit(solution)/shard_map/scatter-add | solution.py:92
  289.8 1.0 gather_fusion.2
  290.8 19.2 %all_to_all.29 = f32[32,8,4,128]{3,2,1,0:T(4,128)S(1)} all-to-all(f32[32,8,4,128]{3,2,1,0:T(4,128)S(1)} %bitcast.54), channel_id=1, replica_groups=mesh['row'=4,'col'=8] {'row','col'}, dimensions={0} | all-to-all | bytes 1048576 | tf_op jit(solution)/shard_map/all_to_all | solution.py:83
  310.0 0.9 gather_fusion.3
  311.2 39.0 %psum.36 = f32[4]{0:T(128)S(1)} all-reduce(f32[4]{0:T(128)S(1)} %multiply_reduce_fusion.3), channel_id=1, replica_groups=mesh['row'=4,'col'=8] {'row','col'}, use_global_device_ids=true, to_apply=%region_10.12 | all-reduce | flops 4 | bytes 32 | tf_op jit(solution)/shard_map/psum | solution.py:128
  350.5 40.0 %psum.37 = f32[4]{0:T(128)S(1)} all-reduce(f32[4]{0:T(128)S(1)} %multiply_reduce_fusion.2), channel_id=1, replica_groups=mesh['row'=4,'col'=8] {'row','col'}, use_global_device_ids=true, to_apply=%region_12.14 | all-reduce | flops 4 | bytes 32 | tf_op jit(solution)/shard_map/psum | solution.py:131
  390.7 5.7 scatter_fusion.5
  396.5 14.6 %all_to_all.30 = bf16[32,8,4,128]{3,2,1,0:T(4,128)(2,1)S(1)} all-to-all(bf16[32,8,4,128]{3,2,1,0:T(4,128)(2,1)S(1)} %scatter_fusion.5), channel_id=1, replica_groups=mesh['row'=4,'col'=8] {'row','col'}, dimensions={0} | all-to-all | bytes 524288 | tf_op jit(solution)/shard_map/all_to_all | solution.py:73
  411.1 7.3 %scatter_fusion.6 = bf16[128,4,128]{2,1,0:T(4,128)(2,1)S(1)} fusion(bf16[128,4,128]{2,1,0:T(4,128)(2,1)S(1)} %broadcast.140, s32[256]{0:T(256)S(1)} %bitcast.58, bf16[256,4,128]{2,1,0:T(4,128)(2,1)S(1)} %bitcast.56), kind=kCustom, calls=%fused_computation.14 | custom fusion | bytes 787456 | tf_op jit(solution)/shard_map/scatter | solution.py:78
  418.5 1.0 collective-permute-start.5
  419.4 6.2 collective-permute-done.5
  425.6 6.8 %collective-permute-done.6 = bf16[128,4,128]{2,1,0:T(4,128)(2,1)S(1)} collective-permute-done((bf16[128,4,128]{2,1,0:T(4,128)(2,1)S(1)}, bf16[128,4,128]{2,1,0:T(4,128)(2,1)S(1)}, u32[]{:S(2)}, u32[]{:S(2)}) %collective-permute-start.6) | collective-permute-done | bytes 131104 | tf_op jit(solution)/shard_map/ppermute | solution.py:96
  432.4 0.4 collective-permute-start.7
  432.8 6.8 %collective-permute-done.7 = bf16[128,4,128]{2,1,0:T(4,128)(2,1)S(1)} collective-permute-done((bf16[128,4,128]{2,1,0:T(4,128)(2,1)S(1)}, bf16[128,4,128]{2,1,0:T(4,128)(2,1)S(1)}, u32[]{:S(2)}, u32[]{:S(2)}) %collective-permute-start.7) | collective-permute-done | bytes 131104 | tf_op jit(solution)/shard_map/ppermute | solution.py:96
  439.5 11.7 %fusion.7 = bf16[512,4,128]{2,1,0:T(4,128)(2,1)S(1)} fusion(s32[]{:T(128)S(6)} %select_n.93, bf16[128,4,128]{2,1,0:T(4,128)(2,1)S(1)} %collective-permute-done.7, bf16[128,4,128]{2,1,0:T(4,128)(2,1)S(1)} %collective-permute-done.6, bf16[128,4,128]{2,1,0:T(4,128)(2,1)S(1)} %collective-permute-done.5, bf16[128,4,128]{2,1,0:T(4,128)(2,1)S(1)} %scatter_fusion.6), kind=kLoop, calls=%fused_computation.42 | loop fusion | flops 1835008 | bytes 1048580 | tf_op jit(solution)/shard_map/jit(_roll_dynamic)/concatenate | solution.py:99
  451.2 3.6 gather_fusion.4
  454.8 8.3 %fusion.1 = f32[1024,4,128]{2,1,0:T(4,128)} fusion(bf16[1024,16,128]{2,1,0:T(8,128)(2,1)} %param.20, bf16[1024,4,128]{2,1,0:T(4,128)(2,1)S(1)} %gather_fusion.4, bf16[1024,16,128]{2,1,0:T(8,128)(2,1)} %param.21, f32[1024,16]{1,0:T(8,128)S(1)} %fusion.18), kind=kOutput, calls=%fused_computation.20 | convolution fusion | flops 33685504 | bytes 11599872 | tf_op jit(solution)/shard_map/etq,etk->eqk/dot_general | solution.py:104
  463.4 66.4 %scatter_fusion.7 = f32[1024,4,128]{2,1,0:T(4,128)S(1)} fusion(f32[1024,4,128]{2,1,0:T(4,128)S(1)} %broadcast.151, s32[1024]{0:T(1024)S(1)} %compare_select_fusion.1, f32[1024,4,128]{2,1,0:T(4,128)} %fusion.1), kind=kCustom, calls=%fused_computation.15 | custom fusion | flops 524288 | bytes 6295552 | tf_op jit(solution)/shard_map/scatter-add | solution.py:110
  529.8 1.3 copy-done
  531.1 1.3 collective-permute-start.9
  532.4 3.0 collective-permute-start.8
  535.5 0.8 collective-permute-done.8
  536.5 2.0 gather_fusion.5
  538.5 9.6 %fusion.35 = f32[384,4,128]{2,1,0:T(4,128)S(1)} fusion(bf16[384,4,128]{2,1,0:T(4,128)(2,1)S(1)} %gather_fusion.5, bf16[384,128,128]{2,1,0:T(8,128)(2,1)} %param.16), kind=kOutput, calls=%fused_computation.109 | convolution fusion | flops 50331648 | bytes 13762560 | tf_op jit(solution)/shard_map/ekp,eqp->eqk/dot_general | solution.py:88
  548.1 41.8 %all-reduce.8.cloned.1.call-done = f32[1024,4,128]{2,1,0:T(4,128)} async-done(((f32[1024,4,128]{2,1,0:T(4,128)}), f32[1024,4,128]{2,1,0:T(4,128)}) %all-reduce.8.cloned.1.call-update) | async-done | bytes 2097168
  589.8 1.0 dynamic-slice_add_fusion
  590.9 14.2 %scatter_fusion.8 = f32[128,4,128]{2,1,0:T(4,128)S(1)} fusion(f32[128,4,128]{2,1,0:T(4,128)S(1)} %dynamic-slice_add_fusion, s32[384]{0:T(512)S(1)} %compare_select_fusion.5, f32[384,4,128]{2,1,0:T(4,128)S(1)} %fusion.35), kind=kCustom, calls=%fused_computation.16 | custom fusion | flops 196608 | bytes 2360832 | tf_op jit(solution)/shard_map/scatter-add | solution.py:92
  605.1 1.0 gather_fusion.6
  606.1 19.2 %all_to_all.31 = f32[32,8,4,128]{3,2,1,0:T(4,128)S(1)} all-to-all(f32[32,8,4,128]{3,2,1,0:T(4,128)S(1)} %bitcast.53), channel_id=1, replica_groups=mesh['row'=4,'col'=8] {'row','col'}, dimensions={0} | all-to-all | bytes 1048576 | tf_op jit(solution)/shard_map/all_to_all | solution.py:83
  625.3 0.9 gather_fusion.7
  626.6 39.0 %all-reduce.2 = (f32[4]{0:T(128)S(1)}, f32[4]{0:T(128)S(1)}) all-reduce(f32[4]{0:T(128)S(1)} %get-tuple-element.17, f32[4]{0:T(128)S(1)} %get-tuple-element.16), channel_id=1, replica_groups=mesh['row'=4,'col'=8] {'row','col'}, use_global_device_ids=true, to_apply=%region_21.23 | all-reduce | flops 8 | bytes 64 | tf_op jit(solution)/shard_map/psum | solution.py:135
  665.6 0.7 copy.19
  666.3 0.9 multiply_subtract_fusion
  (56 shorter events, 3.0 us)
Async XLA Ops:
  7.2 78.3 %copy-start.4 = (s32[1024]{0:T(1024)S(1)}, s32[1024]{0:T(1024)}, u32[]{:S(2)}) copy-start(s32[1024]{0:T(1024)} %param.17) | copy-start | bytes 12292
  7.2 78.3 %copy-start.3 = (s32[1024]{0:T(1024)S(1)}, s32[1024]{0:T(1024)}, u32[]{:S(2)}) copy-start(s32[1024]{0:T(1024)} %param.19) | copy-start | bytes 12292
  14.5 89.8 %copy-start.5 = (s32[1024]{0:T(1024)S(1)}, s32[1024]{0:T(1024)}, u32[]{:S(2)}) copy-start(s32[1024]{0:T(1024)} %param.18) | copy-start | bytes 12292
  14.5 96.0 %copy-start.6 = (s32[384]{0:T(512)S(1)}, s32[384]{0:T(512)}, u32[]{:S(2)}) copy-start(s32[384]{0:T(512)} %param.14) | copy-start | bytes 4612
  14.5 102.9 %copy-start.7 = (s32[384]{0:T(512)S(1)}, s32[384]{0:T(512)}, u32[]{:S(2)}) copy-start(s32[384]{0:T(512)} %param.15) | copy-start | bytes 4612
  14.5 103.0 %copy-start.8 = (u32[32]{0:T(128)S(1)}, u32[32]{0:T(128)}, u32[]{:S(2)}) copy-start(u32[32]{0:T(128)} %constant.163) | copy-start | bytes 388
  16.4 64.5 %all-to-all-start = ((s32[32,1,8]{2,1,0:T(1,128)}), s32[32,1,8]{2,1,0:T(1,128)S(1)}, u32[]{:S(2)}, u32[]{:S(2)}) async-start(s32[32,1,8]{2,1,0:T(1,128)} %copy.18), calls=%async_computation | async-start | bytes 32768 | tf_op jit(solution)/shard_map/all_to_all | solution.py:58
  80.9 15.1 %all-to-all-start.1 = ((bf16[32,8,4,128]{3,2,1,0:T(4,128)(2,1)}), bf16[32,8,4,128]{3,2,1,0:T(4,128)(2,1)S(1)}, u32[]{:S(2)}, u32[]{:S(2)}) async-start(bf16[32,8,4,128]{3,2,1,0:T(4,128)(2,1)} %scatter_fusion.1), calls=%async_computation.1 | async-start | bytes 524288 | tf_op jit(solution)/shard_map/all_to_all | solution.py:73
  85.4 189.1 %all-reduce.6.cloned.1.call-start = ((), (), s32[]{:S(2)}) async-start(), calls=%async_computation.5 | async-start | bytes 4194304
  103.4 7.2 %collective-permute-start = (bf16[128,4,128]{2,1,0:T(4,128)(2,1)S(1)}, bf16[128,4,128]{2,1,0:T(4,128)(2,1)S(1)}, u32[]{:S(2)}, u32[]{:S(2)}) collective-permute-start(bf16[128,4,128]{2,1,0:T(4,128)(2,1)S(1)} %scatter_fusion.2), channel_id=1, source_target_pairs={{0,8},{8,16},{16,24},{24,0},{1,9},{9,17},{17,25},{25,1},{2,10},{10... | collective-permute-start | bytes 393224 | tf_op jit(solution)/shard_map/ppermute | solution.py:96
  110.5 6.8 %collective-permute-start.1 = (bf16[128,4,128]{2,1,0:T(4,128)(2,1)S(1)}, bf16[128,4,128]{2,1,0:T(4,128)(2,1)S(1)}, u32[]{:S(2)}, u32[]{:S(2)}) collective-permute-start(bf16[128,4,128]{2,1,0:T(4,128)(2,1)S(1)} %collective-permute-done), channel_id=1, source_target_pairs={{0,8},{8,16},{16,24},{24,0},{1,9},{9,17},{17,25},{25,1},{2,10},{10... | collective-permute-start | bytes 393224 | tf_op jit(solution)/shard_map/ppermute | solution.py:96
  117.3 6.9 %collective-permute-start.2 = (bf16[128,4,128]{2,1,0:T(4,128)(2,1)S(1)}, bf16[128,4,128]{2,1,0:T(4,128)(2,1)S(1)}, u32[]{:S(2)}, u32[]{:S(2)}) collective-permute-start(bf16[128,4,128]{2,1,0:T(4,128)(2,1)S(1)} %collective-permute-done.1), channel_id=1, source_target_pairs={{0,8},{8,16},{16,24},{24,0},{1,9},{9,17},{17,25},{25,1},{2,10},{10... | collective-permute-start | bytes 393224 | tf_op jit(solution)/shard_map/ppermute | solution.py:96
  214.5 1.3 copy-start.1
  215.8 374.0 %all-reduce.8.cloned.1.call-start = ((), (), s32[]{:S(2)}) async-start(), calls=%async_computation.6 | async-start | bytes 4194304
  215.9 4.4 collective-permute-start.4
  217.2 3.9 collective-permute-start.3
  390.7 275.6 %copy-start.2 = (f32[128,4,128]{2,1,0:T(4,128)}, f32[128,4,128]{2,1,0:T(4,128)S(1)}, u32[]{:S(2)}) copy-start(f32[128,4,128]{2,1,0:T(4,128)S(1)} %get-tuple-element.21) | copy-start | bytes 786436
  418.5 7.2 %collective-permute-start.5 = (bf16[128,4,128]{2,1,0:T(4,128)(2,1)S(1)}, bf16[128,4,128]{2,1,0:T(4,128)(2,1)S(1)}, u32[]{:S(2)}, u32[]{:S(2)}) collective-permute-start(bf16[128,4,128]{2,1,0:T(4,128)(2,1)S(1)} %scatter_fusion.6), channel_id=1, source_target_pairs={{0,8},{8,16},{16,24},{24,0},{1,9},{9,17},{17,25},{25,1},{2,10},{10... | collective-permute-start | bytes 393224 | tf_op jit(solution)/shard_map/ppermute | solution.py:96
  425.6 6.8 %collective-permute-start.6 = (bf16[128,4,128]{2,1,0:T(4,128)(2,1)S(1)}, bf16[128,4,128]{2,1,0:T(4,128)(2,1)S(1)}, u32[]{:S(2)}, u32[]{:S(2)}) collective-permute-start(bf16[128,4,128]{2,1,0:T(4,128)(2,1)S(1)} %collective-permute-done.5), channel_id=1, source_target_pairs={{0,8},{8,16},{16,24},{24,0},{1,9},{9,17},{17,25},{25,1},{2,10},{10... | collective-permute-start | bytes 393224 | tf_op jit(solution)/shard_map/ppermute | solution.py:96
  432.4 7.1 %collective-permute-start.7 = (bf16[128,4,128]{2,1,0:T(4,128)(2,1)S(1)}, bf16[128,4,128]{2,1,0:T(4,128)(2,1)S(1)}, u32[]{:S(2)}, u32[]{:S(2)}) collective-permute-start(bf16[128,4,128]{2,1,0:T(4,128)(2,1)S(1)} %collective-permute-done.6), channel_id=1, source_target_pairs={{0,8},{8,16},{16,24},{24,0},{1,9},{9,17},{17,25},{25,1},{2,10},{10... | collective-permute-start | bytes 393224 | tf_op jit(solution)/shard_map/ppermute | solution.py:96
  529.8 1.3 copy-start
  531.1 4.3 collective-permute-start.9
  532.4 3.9 collective-permute-start.8
Sparse Core Ops, SparseCore 0:
  215.9 58.5 all-reduce.5
  531.2 58.5 all-reduce.7
